TPU v7x, 256 devices: a whole 4x4x8 slice. The times are simulated.
256 devices in a mesh: rows: 32 (over z_hi, y, x), cols: 8 (over z_lo, core).
Axes of the slice: x: 4, y: 4, z: 8 (z_hi: 2, z_lo: 4; z = z_hi * 4 + z_lo), core: 2. Of those that a mesh axis runs over, the one named last changes fastest.
Arguments:
- logged: bfloat16 [32768, 256], P(('rows', 'cols')), may hold values from -8 to 8
- fresh: bfloat16 [65536, 256], P(('cols', 'rows')), may hold values from -6 to 6
- warm: float32 [65536], P('cols'), may hold values from -1 to 1
Outputs:
- row_potential: float32 [32768], P('rows')
- col_potential: float32 [65536], P('cols')
- reward: float32 [32768], P('rows')
All inputs are finite; a program needn't handle non-finite values.
Results may differ from a plain program's by a relative error of at most 0.0013.
Values may be sent and summed in bfloat16 or wider, within the bound.
No kernel may reach another device: no remote copies, remote signals or barrier semaphores. Data moves between devices by JAX's collectives and lax.ppermute only.
A program may use at most 128 MiB of HBM per device.

v0:
```python
import jax
import jax.numpy as jnp
from jax import lax
from jax.sharding import PartitionSpec as P

EPS = 0.01


def body(logged, fresh, warm):
    block = lax.all_gather(logged, "cols", axis=0, tiled=True)
    wide = block.astype(jnp.float32)
    block_sq = jnp.sum(wide * wide, axis=1)
    width = block.shape[1]
    total_rows = block.shape[0] * lax.axis_size("rows")
    total_cols = warm.shape[0] * lax.axis_size("cols")
    piece = lax.all_gather(fresh, "rows", axis=0, tiled=True)
    piece_wide = piece.astype(jnp.float32)
    piece_sq = jnp.sum(piece_wide * piece_wide, axis=1)
    inner = lax.dot_general(
        block, piece, (((1,), (1,)), ((), ())), preferred_element_type=jnp.float32
    )
    stored = (block_sq[:, None] + piece_sq[None, :] - 2.0 * inner) / width

    def get_tile():
        return stored

    expo = (warm[None, :] - get_tile()) / EPS
    top = jnp.max(expo, axis=1)
    total = jnp.sum(jnp.exp(expo - top[:, None]), axis=1)
    both = lax.pmax(top, "cols")
    total = lax.psum(total * jnp.exp(top - both), "cols")
    top = both
    row_potential = -EPS * (top + jnp.log(total)) - EPS * jnp.log(jnp.float32(total_rows))
    expo = (row_potential[:, None] - get_tile()) / EPS
    top = jnp.max(expo, axis=0)
    total = jnp.sum(jnp.exp(expo - top[None, :]), axis=0)
    both = lax.pmax(top.astype(jnp.bfloat16), "rows").astype(top.dtype)
    total = lax.psum(total * jnp.exp(top - both), "rows")
    top = both
    col_potential = -EPS * (top + jnp.log(total)) - EPS * jnp.log(jnp.float32(total_cols))
    cost = get_tile()
    plan = jnp.exp((row_potential[:, None] + col_potential[None, :] - cost) / EPS)
    partial_cost = jnp.sum(plan * cost, axis=1)
    reward = -jnp.float32(total_rows) * lax.psum(partial_cost, "cols")
    return (row_potential, col_potential, reward)


def solution(mesh):
    return jax.shard_map(
        body,
        mesh=mesh,
        in_specs=(P(("rows", "cols"), None), P(("cols", "rows"), None), P("cols")),
        out_specs=(P("rows"), P("cols"), P("rows")),
        check_vma=False,
    )
```

profile of v0, /device:TPU:1, one launch (start us, length us, event | category | flops | bytes accessed | tf_op | source)
XLA Modules:
  0.0 682.2 jit_solution(6621677491578648344)
XLA Ops:
  7.2 0.0 all-gather.2.cloned.1.call-start
  7.2 0.7 all-gather.2.cloned.1.call-update
  7.9 18.0 %all_gather.6 = bf16[1024,256]{1,0:T(8,128)(2,1)S(1)} all-gather(bf16[128,256]{1,0:T(8,128)(2,1)} %param.3), channel_id=1, replica_groups=mesh['rows'=32,'cols'=8] {'cols'}, dimensions={0}, use_global_device_ids=true | all-gather | bytes 589824 | tf_op jit(solution)/shard_map/all_gather | solution.py:10
  25.9 0.2 multiply_reduce_fusion.2
  26.1 96.6 %all-gather.2.cloned.1.call-done = bf16[8192,256]{1,0:T(8,128)(2,1)} async-done(((bf16[256,256]{1,0:T(8,128)(2,1)}), bf16[8192,256]{1,0:T(8,128)(2,1)}) %all-gather.2.cloned.1.call-update) | async-done | bytes 4194320 | tf_op jit(solution)/shard_map/all_gather | solution.py:16
  122.7 3.3 multiply_reduce_fusion.1
  126.0 0.0 copy-start.2
  126.1 15.9 %fusion = (f32[1024]{0:T(1024)S(1)}, f32[1024,8192]{1,0:T(8,128)}) fusion(f32[8192]{0:T(1024)} %param.5, bf16[1024,256]{1,0:T(8,128)(2,1)S(1)} %all_gather.6, bf16[8192,256]{1,0:T(8,128)(2,1)} %all-gather.2.cloned.1.call-done, f32[8192]{0:T(1024)S(1)} %multiply_reduce_fusion.1, f32[1024]{0:T(1024)S(1)} %multiply_reduce_fusion.2), kind=kOutput, calls=%fused_computation.6 | convolution fusion | flops 4353686528 | bytes 38346752 | tf_op jit(solution)/shard_map/dot_general | solution.py:19
  142.0 17.9 %pmax.14 = f32[1024]{0:T(1024)S(1)} all-reduce(f32[1024]{0:T(1024)S(1)} %get-tuple-element.3), channel_id=1, replica_groups=mesh['rows'=32,'cols'=8] {'cols'}, use_global_device_ids=true, to_apply=%region_3.0 | all-reduce | flops 1024 | bytes 8192 | tf_op jit(solution)/shard_map/pmax | solution.py:30
  159.9 0.0 copy-done.2
  159.9 14.7 %exponential_reduce_fusion.1 = f32[1024]{0:T(1024)S(1)} fusion(f32[1024,8192]{1,0:T(8,128)} %get-tuple-element.4, f32[1024]{0:T(1024)S(1)} %get-tuple-element.3, f32[8192]{0:T(1024)S(1)} %copy-done.2), kind=kLoop, calls=%fused_computation.3 | loop fusion | flops 33553408 | bytes 33595392 | tf_op jit(solution)/shard_map/reduce_sum | solution.py:29
  174.7 13.6 %psum.21 = f32[1024]{0:T(1024)S(1)} all-reduce(f32[1024]{0:T(1024)S(1)} %exponential_multiply_fusion), channel_id=1, replica_groups=mesh['rows'=32,'cols'=8] {'cols'}, use_global_device_ids=true, to_apply=%region_5.0 | all-reduce | flops 1024 | bytes 8192 | tf_op jit(solution)/shard_map/psum | solution.py:31
  188.3 0.0 copy-start.1
  188.3 12.9 %fusion.1 = f32[8192]{0:T(1024)S(1)} fusion(f32[1024,8192]{1,0:T(8,128)} %get-tuple-element.4, f32[1024]{0:T(1024)S(1)} %multiply_add_fusion), kind=kLoop, calls=%fused_computation.7 | loop fusion | flops 25157632 | bytes 33591296 | tf_op jit(solution)/shard_map/reduce_max | solution.py:35
  201.2 14.5 %exponential_reduce_fusion = f32[8192]{0:T(1024)S(1)} fusion(f32[1024,8192]{1,0:T(8,128)} %get-tuple-element.4, f32[8192]{0:T(1024)S(1)} %fusion.1, f32[1024]{0:T(1024)S(1)} %multiply_add_fusion), kind=kLoop, calls=%fused_computation.1 | loop fusion | flops 33546240 | bytes 33624064 | tf_op jit(solution)/shard_map/reduce_sum | solution.py:36
  215.7 187.5 %pmax.15 = bf16[8192]{0:T(1024)(128)(2,1)S(1)} all-reduce(bf16[8192]{0:T(1024)(128)(2,1)S(1)} %convert_element_type.14), channel_id=1, replica_groups=mesh['rows'=32,'cols'=8] {'rows'}, use_global_device_ids=true, to_apply=%region_7.0 | all-reduce | flops 8192 | bytes 32768 | tf_op jit(solution)/shard_map/pmax | solution.py:37
  403.2 187.1 %psum.22 = f32[8192]{0:T(1024)S(1)} all-reduce(f32[8192]{0:T(1024)S(1)} %fusion.3), channel_id=1, replica_groups=mesh['rows'=32,'cols'=8] {'rows'}, use_global_device_ids=true, to_apply=%region_9.0 | all-reduce | flops 8192 | bytes 65536 | tf_op jit(solution)/shard_map/psum | solution.py:38
  590.4 0.0 copy-done.1
  590.4 0.0 copy-start
  590.4 15.1 %multiply_reduce_fusion = f32[1024]{0:T(1024)S(1)} fusion(f32[1024,8192]{1,0:T(8,128)} %get-tuple-element.4, f32[8192]{0:T(1024)S(1)} %fusion.5, f32[1024]{0:T(1024)S(1)} %multiply_add_fusion), kind=kLoop, calls=%fused_computation | loop fusion | flops 41942016 | bytes 33595392 | tf_op jit(solution)/shard_map/reduce_sum | solution.py:43
  605.5 69.3 %psum.23 = f32[1024]{0:T(1024)S(1)} all-reduce(f32[1024]{0:T(1024)S(1)} %multiply_reduce_fusion), channel_id=1, replica_groups=mesh['rows'=32,'cols'=8] {'cols'}, use_global_device_ids=true, to_apply=%region_11.0 | all-reduce | flops 1024 | bytes 8192 | tf_op jit(solution)/shard_map/psum | solution.py:44
  674.7 0.6 broadcast_multiply_fusion
  675.3 0.0 copy-done
  (5 shorter events, 0.1 us)
Async XLA Ops:
  7.2 115.5 %all-gather.2.cloned.1.call-start = ((), (), s32[]{:S(2)}) async-start(), calls=%async_computation | async-start | bytes 4325376 | tf_op jit(solution)/shard_map/all_gather | solution.py:16
  126.0 33.9 %copy-start.2 = (f32[8192]{0:T(1024)S(1)}, f32[8192]{0:T(1024)}, u32[]{:S(2)}) copy-start(f32[8192]{0:T(1024)} %param.5) | copy-start | bytes 98308
  188.3 402.1 %copy-start.1 = (f32[1024]{0:T(1024)}, f32[1024]{0:T(1024)S(1)}, u32[]{:S(2)}) copy-start(f32[1024]{0:T(1024)S(1)} %multiply_add_fusion) | copy-start | bytes 12292
  590.4 85.0 %copy-start = (f32[8192]{0:T(1024)}, f32[8192]{0:T(1024)S(1)}, u32[]{:S(2)}) copy-start(f32[8192]{0:T(1024)S(1)} %fusion.5) | copy-start | bytes 98308
Sparse Core Ops, SparseCore 0:
  11.4 111.2 all-gather.1
where the time goes:
time: 683 us; the launch traced here: 682 us
  blocking collectives  493 us (72%)
  waiting for transfers between devices  97.3 us (14%)
  other arithmetic  61.4 us (9%)
  matrix products  15.9 us (2%)
  between operations  14.1 us (2%)
    pmax x1, blocking collectives, body(): both = lax.pmax(top.astype(jnp.bfloat16), 'rows').astype(top.dtype)  188 us
    psum x1, blocking collectives, body(): total = lax.psum(total * jnp.exp(top - both), 'rows')  187 us
    all_gather x1, waiting for transfers between devices, body(): piece = lax.all_gather(fresh, 'rows', axis=0, tiled=True)  96.6 us
    psum x1, blocking collectives, body(): reward = -jnp.float32(total_rows) * lax.psum(partial_cost, 'cols')  69.3 us
    all_gather x1, blocking collectives, body(): block = lax.all_gather(logged, 'cols', axis=0, tiled=True)  18 us
    pmax x1, blocking collectives, body(): both = lax.pmax(top, 'cols')  17.9 us
    dot_general x1, matrix products, body(): lax.dot_general(block, piece, (((1,), (1,)), ((), ())), preferred_element...  15.9 us
    reduce_sum x1, other arithmetic, body(): partial_cost = jnp.sum(plan * cost, axis=1)  15.1 us
  transfers between devices with their start and end apart: 1, of which 1 were waited for; matrix products, arithmetic and copies ran while one was open for 0% of the time, Pallas kernels for 0%

commit v1 on v0

v1 whole, which is shorter than its diff:
```python
import functools
import math

import jax
import jax.numpy as jnp
from jax import lax
from jax.experimental import pallas as pl
from jax.experimental.pallas import tpu as pltpu
from jax.sharding import Mesh
from jax.sharding import PartitionSpec as P

EPS = 0.01
AXES = ("zh", "y", "x", "zl", "core")
ROW_GROUP = ("zh", "zl", "core")
COL_GROUP = ("y", "x")
LN2 = math.log(2.0)
LOG2E = 1.0 / LN2


def nt_dot(a, b):
    return lax.dot_general(a, b, (((1,), (1,)), ((), ())), preferred_element_type=jnp.float32)


def lse_kernel(scale, width, x_ref, y_ref, bias_ref, out_ref):
    x = x_ref[...]
    tm = x.shape[0]
    top = None
    total = None
    for start in range(0, y_ref.shape[0], width):
        prod = nt_dot(x, y_ref[start : start + width, :])
        parts = [
            prod[:, o : o + 128] * scale + bias_ref[:, start + o : start + o + 128]
            for o in range(0, width, 128)
        ]
        new = functools.reduce(jnp.maximum, parts)
        if top is not None:
            new = jnp.maximum(new, top)
        add = functools.reduce(jnp.add, [jnp.exp2(p - new) for p in parts])
        total = add if top is None else total * jnp.exp2(top - new) + add
        top = new
    top = top.T
    total = total.T
    best = jnp.max(top, axis=0, keepdims=True)
    out_ref[...] = best + jnp.log2(jnp.sum(total * jnp.exp2(top - best), axis=0, keepdims=True))


def lse(x, y, bias, scale, tm=256, width=1024):
    rows, depth = x.shape
    cols = y.shape[0]
    return pl.pallas_call(
        functools.partial(lse_kernel, scale, width),
        grid=(rows // tm,),
        in_specs=[
            pl.BlockSpec((tm, depth), lambda i: (i, 0)),
            pl.BlockSpec((cols, depth), lambda i: (0, 0)),
            pl.BlockSpec((1, cols), lambda i: (0, 0)),
        ],
        out_specs=pl.BlockSpec((1, tm), lambda i: (0, i)),
        out_shape=jax.ShapeDtypeStruct((1, rows), jnp.float32),
        compiler_params=pltpu.CompilerParams(vmem_limit_bytes=40 * 2**20),
        cost_estimate=pl.CostEstimate(
            flops=2 * rows * cols * depth, bytes_accessed=2 * depth * (rows + cols), transcendentals=rows * cols
        ),
    )(x, y, bias)


def reward_kernel(scale, width, x_ref, y_ref, rbias_ref, rsq_ref, cbias_ref, csq_ref, out_ref):
    x = x_ref[...]
    tm = x.shape[0]
    rbias = jnp.broadcast_to(rbias_ref[...], (128, tm)).T
    mass = jnp.zeros((tm, 128), jnp.float32)
    moment = jnp.zeros((tm, 128), jnp.float32)
    for start in range(0, y_ref.shape[0], width):
        prod = nt_dot(x, y_ref[start : start + width, :])
        for o in range(0, width, 128):
            part = prod[:, o : o + 128]
            cols = slice(start + o, start + o + 128)
            plan = jnp.exp2((part * scale + cbias_ref[:, cols]) + rbias)
            mass = mass + plan
            moment = moment + plan * (part - csq_ref[:, cols])
    mass = jnp.sum(mass.T, axis=0, keepdims=True)
    moment = jnp.sum(moment.T, axis=0, keepdims=True)
    out_ref[...] = rsq_ref[...] * mass - 2.0 * moment


def reward_part(x, y, rbias, rsq, cbias, csq, scale, tm=256, width=1024):
    rows, depth = x.shape
    cols = y.shape[0]
    return pl.pallas_call(
        functools.partial(reward_kernel, scale, width),
        grid=(rows // tm,),
        in_specs=[
            pl.BlockSpec((tm, depth), lambda i: (i, 0)),
            pl.BlockSpec((cols, depth), lambda i: (0, 0)),
            pl.BlockSpec((1, tm), lambda i: (0, i)),
            pl.BlockSpec((1, tm), lambda i: (0, i)),
            pl.BlockSpec((1, cols), lambda i: (0, 0)),
            pl.BlockSpec((1, cols), lambda i: (0, 0)),
        ],
        out_specs=pl.BlockSpec((1, tm), lambda i: (0, i)),
        out_shape=jax.ShapeDtypeStruct((1, rows), jnp.float32),
        compiler_params=pltpu.CompilerParams(vmem_limit_bytes=40 * 2**20),
        cost_estimate=pl.CostEstimate(
            flops=2 * rows * cols * depth, bytes_accessed=2 * depth * (rows + cols), transcendentals=rows * cols
        ),
    )(x, y, rbias, rsq, cbias, csq)


def share(a, axes):
    n = math.prod(lax.axis_size(ax) for ax in axes)
    return lax.all_to_all(jnp.broadcast_to(a[None], (n,) + a.shape), axes, 0, 0)


def merge(parts):
    best = jnp.max(parts, axis=0)
    return best + jnp.log2(jnp.sum(jnp.exp2(parts - best), axis=0))


def body(logged, fresh, warm):
    depth = logged.shape[1]
    zh = lax.axis_index("zh")
    n_rows = logged.shape[0] * 256
    n_cols = fresh.shape[0] * 256

    mine = share(logged, ("zh", "zl"))
    other = lax.ppermute(mine, "core", [(0, 1), (1, 0)])
    core = lax.axis_index("core")
    even = jnp.where(core == 0, mine, other)
    odd = jnp.where(core == 0, other, mine)
    x = jnp.stack([even, odd], axis=1).reshape(-1, depth)
    y = share(fresh, COL_GROUP).reshape(-1, depth)
    rows, cols = x.shape[0], y.shape[0]

    scale = 2.0 * LOG2E / (depth * EPS)
    xw = x.astype(jnp.float32)
    xsq = jnp.sum(xw * xw, axis=1)
    yw = y.astype(jnp.float32)
    ysq = jnp.sum(yw * yw, axis=1)
    warm = lax.dynamic_slice(warm, (zh * cols,), (cols,))

    bias = warm * (LOG2E / EPS) - ysq * (0.5 * scale)
    part = lse(x, y, bias[None], scale)
    total = merge(share(part.reshape(-1), ROW_GROUP))
    rbias = -total - math.log2(n_rows)
    row_all = (rbias + xsq * (0.5 * scale)) * (EPS * LN2)

    part = lse(y, x, rbias[None], scale)
    total = merge(share(part.reshape(-1), COL_GROUP))
    cbias = -total - math.log2(n_cols)
    col_half = (cbias + ysq * (0.5 * scale)) * (EPS * LN2)
    theirs = lax.ppermute(col_half, "zh", [(0, 1), (1, 0)])
    col_potential = jnp.where(
        zh == 0, jnp.concatenate([col_half, theirs]), jnp.concatenate([theirs, col_half])
    )

    part = reward_part(x, y, rbias[None], xsq[None], cbias[None], (0.5 * ysq)[None], scale)
    halves = part.reshape(2, rows // 2)
    sent = jnp.broadcast_to(halves[:, None], (2, 8, rows // 2)).reshape(16, rows // 2)
    got = lax.all_to_all(sent, ROW_GROUP, 0, 0)
    reward = jnp.sum(got, axis=0) * (-n_rows / depth)
    row_potential = lax.dynamic_slice(row_all, (zh * (rows // 2),), (rows // 2,))
    return row_potential, col_potential, reward


def solution(mesh):
    fine = Mesh(mesh.devices.reshape(2, 4, 4, 4, 2), AXES)
    return jax.shard_map(
        body,
        mesh=fine,
        in_specs=(P(AXES, None), P(("zl", "core", "zh", "y", "x"), None), P(("zl", "core"))),
        out_specs=(P(("zh", "y", "x")), P(("zl", "core")), P(("zh", "y", "x"))),
        check_vma=False,
    )
```

time: 683 us -> 146 us (0.21)
  blocking collectives: 493 us -> 24.8 us
  waiting for transfers between devices: 97.3 us -> 40.1 us
  other arithmetic: 61.4 us -> 5.47 us
  Pallas kernels: 0 us -> 35.6 us
  starting transfers between devices: 0.04 us -> 31.6 us
  matrix products: 15.9 us -> 0 us
  between operations: 14.1 us -> 0.82 us
  local copies, waits for them, and re-layouts: 0.02 us -> 7.17 us
    psum x3 -> x0, blocking collectives: 270 us -> none  [the longest x1 187 us: body(): total = lax.psum(total * jnp.exp(top - both), 'rows')]
    pmax x2 -> x0, blocking collectives: 205 us -> none  [the longest x1 188 us: body(): both = lax.pmax(top.astype(jnp.bfloat16), 'rows').astype(top.dtype)]
    all_gather x1 -> x0, waiting for transfers between devices: 96.6 us -> none  [body(): piece = lax.all_gather(fresh, 'rows', axis=0, tiled=True)]
    reduce_sum x5, other arithmetic: 47.8 us -> 2.5 us  [the longest x1 1.56 us: body(): xsq = jnp.sum(xw * xw, axis=1)]
    all_to_all x0 -> x4, waiting for transfers between devices: none -> 36.5 us  [the longest x3 36.5 us: share(): return lax.all_to_all(jnp.broadcast_to(a[None], (n,) + a.shape), axes, 0, 0)]
    pallas_call x0 -> x3, Pallas kernels: none -> 35.6 us  [the longest x2 23.1 us: lse(): pl.pallas_call(functools.partial(lse_kernel, scale, width), grid=(rows //...]
    all_to_all x0 -> x1, blocking collectives: none -> 24.8 us  [share(): return lax.all_to_all(jnp.broadcast_to(a[None], (n,) + a.shape), axes, 0, 0)]
    all_to_all x0 -> x4, starting transfers between devices: none -> 23.5 us  [the longest x3 19.6 us: share(): return lax.all_to_all(jnp.broadcast_to(a[None], (n,) + a.shape), axes, 0, 0)]
  transfers between devices with their start and end apart: 1 -> 6, of which waited for: 1 -> 5; matrix products, arithmetic and copies ran while one was open for 0% -> 2% of each run, Pallas kernels for 0% -> 0%
where the time goes in v1:
time: 146 us
  waiting for transfers between devices  40.1 us (27%)
  Pallas kernels  35.6 us (24%)
  starting transfers between devices  31.6 us (22%)
  blocking collectives  24.8 us (17%)
  local copies, waits for them, and re-layouts  7.17 us (5%)
  other arithmetic  5.47 us (4%)
    all_to_all x3, waiting for transfers between devices, share(): return lax.all_to_all(jnp.broadcast_to(a[None], (n,) + a.shape), axes, 0, 0)  36.5 us
    all_to_all x1, blocking collectives, share(): return lax.all_to_all(jnp.broadcast_to(a[None], (n,) + a.shape), axes, 0, 0)  24.8 us
    pallas_call x2, Pallas kernels, lse(): pl.pallas_call(functools.partial(lse_kernel, scale, width), grid=(rows //...  23.1 us
    all_to_all x3, starting transfers between devices, share(): return lax.all_to_all(jnp.broadcast_to(a[None], (n,) + a.shape), axes, 0, 0)  19.6 us
    pallas_call x1, Pallas kernels, reward_part(): pl.pallas_call(functools.partial(reward_kernel, scale, width), grid=(rows...  12.5 us
    ppermute x1, starting transfers between devices, body(): theirs = lax.ppermute(col_half, 'zh', [(0, 1), (1, 0)])  5.34 us
    broadcast_in_dim x4, local copies, waits for them, and re-layouts, share(): return lax.all_to_all(jnp.broadcast_to(a[None], (n,) + a.shape), axes, 0, 0)  4.93 us
    all_to_all x1, starting transfers between devices, body(): got = lax.all_to_all(sent, ROW_GROUP, 0, 0)  3.81 us
  transfers between devices with their start and end apart: 6, of which 5 were waited for; matrix products, arithmetic and copies ran while one was open for 2% of the time, Pallas kernels for 0%

profile of v1, /device:TPU:1, one launch (start us, length us, event | category | flops | bytes accessed | tf_op | source)
XLA Modules:
  0.0 145.6 jit_solution(13779720044338836103)
XLA Ops:
  0.6 0.9 broadcast_in_dim.16
  1.5 24.8 %all_to_all.37 = bf16[8,128,256]{2,1,0:T(8,128)(2,1)S(1)} all-to-all(bf16[8,128,256]{2,1,0:T(8,128)(2,1)S(1)} %broadcast_in_dim.16), channel_id=1, replica_groups=mesh['zh'=2,'y'=4,'x'=4,'zl'=4,'core'=2] {'zh','zl'}, dimensions={0} | all-to-all | bytes 1048576 | tf_op jit(solution)/shard_map/all_to_all | solution.py:111
  26.3 2.5 %broadcast_in_dim.17 = bf16[16,256,256]{2,1,0:T(8,128)(2,1)} broadcast(bf16[256,256]{1,0:T(8,128)(2,1)} %param.4), dimensions={1,2} | broadcast | bytes 2228224 | tf_op jit(solution)/shard_map/broadcast_in_dim | solution.py:111
  28.8 6.8 %all-to-all-start.1 = ((bf16[16,256,256]{2,1,0:T(8,128)(2,1)}), bf16[16,256,256]{2,1,0:T(8,128)(2,1)S(1)}, u32[]{:S(2)}, u32[]{:S(2)}) async-start(bf16[16,256,256]{2,1,0:T(8,128)(2,1)} %broadcast_in_dim.17), calls=%async_computation.1 | async-start | bytes 4194304 | tf_op jit(solution)/shard_map/all_to_all | solution.py:111
  35.5 2.8 %collective-permute-start = (bf16[8,128,256]{2,1,0:T(8,128)(2,1)S(1)}, bf16[8,128,256]{2,1,0:T(8,128)(2,1)S(1)}, u32[]{:S(2)}, u32[]{:S(2)}) collective-permute-start(bf16[8,128,256]{2,1,0:T(8,128)(2,1)S(1)} %all_to_all.37), channel_id=1, source_target_pairs={{0,1},{1,0},{2,3},{3,2},{4,5},{5,4},{6,7},{7,6},{8,9},{9,8},{10,11... | collective-permute-start | bytes 1572872 | tf_op jit(solution)/shard_map/ppermute | solution.py:126
  38.4 1.5 %collective-permute-done = bf16[8,128,256]{2,1,0:T(8,128)(2,1)S(1)} collective-permute-done((bf16[8,128,256]{2,1,0:T(8,128)(2,1)S(1)}, bf16[8,128,256]{2,1,0:T(8,128)(2,1)S(1)}, u32[]{:S(2)}, u32[]{:S(2)}) %collective-permute-start) | collective-permute-done | bytes 524320 | tf_op jit(solution)/shard_map/ppermute | solution.py:126
  40.0 0.8 copy-done
  40.8 0.2 copy-done.1
  41.0 0.1 pad_maximum_fusion
  41.1 19.9 %all-to-all-done.1 = bf16[16,256,256]{2,1,0:T(8,128)(2,1)S(1)} async-done(((bf16[16,256,256]{2,1,0:T(8,128)(2,1)}), bf16[16,256,256]{2,1,0:T(8,128)(2,1)S(1)}, u32[]{:S(2)}, u32[]{:S(2)}) %all-to-all-start.1) | async-done | bytes 2097184 | tf_op jit(solution)/shard_map/all_to_all | solution.py:111
  61.0 0.6 multiply_reduce_fusion
  61.6 10.6 %shard_map.58 = f32[1,2048]{1,0:T(1,128)S(1)} custom-call(bf16[2048,256]{1,0:T(8,128)(2,1)S(1)} %bitcast.41, bf16[4096,256]{1,0:T(8,128)(2,1)S(1)} %bitcast.38, f32[1,4096]{1,0:T(1,128)S(1)} %bitcast.48), custom_call_target="tpu_custom_call" | custom-call | flops 4294967296 | bytes 3145728 | tf_op jit(solution)/shard_map/pallas_call | solution.py:50
  72.2 0.7 broadcast_in_dim.19
  72.9 9.4 %all-to-all-start.2 = ((f32[16,1,2048]{2,1,0:T(1,128)}), f32[16,1,2048]{2,1,0:T(1,128)S(1)}, u32[]{:S(2)}, u32[]{:S(2)}) async-start(f32[16,1,2048]{2,1,0:T(1,128)} %broadcast_in_dim.19), calls=%async_computation.2 | async-start | bytes 262144 | tf_op jit(solution)/shard_map/all_to_all | solution.py:111
  82.3 9.2 %all-to-all-done.2 = f32[16,1,2048]{2,1,0:T(1,128)S(1)} async-done(((f32[16,1,2048]{2,1,0:T(1,128)}), f32[16,1,2048]{2,1,0:T(1,128)S(1)}, u32[]{:S(2)}, u32[]{:S(2)}) %all-to-all-start.2) | async-done | bytes 131104 | tf_op jit(solution)/shard_map/all_to_all | solution.py:111
  91.7 12.5 %shard_map.59 = f32[1,4096]{1,0:T(1,128)S(1)} custom-call(bf16[4096,256]{1,0:T(8,128)(2,1)S(1)} %bitcast.39, bf16[2048,256]{1,0:T(8,128)(2,1)S(1)} %bitcast.42, f32[1,2048]{1,0:T(1,128)S(1)} %bitcast.45), custom_call_target="tpu_custom_call" | custom-call | flops 4294967296 | bytes 3145728 | tf_op jit(solution)/shard_map/pallas_call | solution.py:50
  104.2 0.9 broadcast_in_dim.20
  105.1 3.5 %all-to-all-start.3 = ((f32[16,1,4096]{2,1,0:T(1,128)}), f32[16,1,4096]{2,1,0:T(1,128)S(1)}, u32[]{:S(2)}, u32[]{:S(2)}) async-start(f32[16,1,4096]{2,1,0:T(1,128)} %broadcast_in_dim.20), calls=%async_computation.3 | async-start | bytes 524288 | tf_op jit(solution)/shard_map/all_to_all | solution.py:111
  108.7 1.6 %multiply_reduce_fusion.1 = f32[8,2,128]{2,1,0:T(2,128)S(1)} fusion(bf16[8,1,128,256]{3,2,1,0:T(8,128)(2,1)} %copy-done.1, bf16[8,1,128,256]{3,2,1,0:T(8,128)(2,1)} %copy-done), kind=kLoop, calls=%fused_computation.1 | loop fusion | flops 2095104 | bytes 1056768 | tf_op jit(solution)/shard_map/reduce_sum | solution.py:136
  110.3 7.5 %all-to-all-done.3 = f32[16,1,4096]{2,1,0:T(1,128)S(1)} async-done(((f32[16,1,4096]{2,1,0:T(1,128)}), f32[16,1,4096]{2,1,0:T(1,128)S(1)}, u32[]{:S(2)}, u32[]{:S(2)}) %all-to-all-start.3) | async-done | bytes 262176 | tf_op jit(solution)/shard_map/all_to_all | solution.py:111
  117.7 0.2 reduce_max.19
  117.9 0.2 fusion.2
  118.1 12.5 %shard_map.60 = f32[1,2048]{1,0:T(1,128)S(1)} custom-call(bf16[2048,256]{1,0:T(8,128)(2,1)S(1)} %bitcast.43, bf16[4096,256]{1,0:T(8,128)(2,1)S(1)} %bitcast.40, f32[1,2048]{1,0:T(1,128)S(1)} %bitcast.46, f32[1,2048]{1,0:T(1,128)S(1)} %bitcast.44, f32[1,4096]{1,0:T(1,128)S(1)} %bitcast.47, f32[1,4096]{1,0:T(1,128)S(1)} %bitcast.50), custom_call_target="tpu_custom_call" | custom-call | flops 4294967296 | bytes 3145728 | tf_op jit(solution)/shard_map/pallas_call | solution.py:89
  130.6 0.5 broadcast.85
  131.1 0.7 reduce.8
  131.8 0.7 all_to_all.30
  132.5 3.8 %all-to-all-start.4 = ((f32[16,1,1024]{2,1,0:T(1,128)}), f32[16,1,1024]{2,1,0:T(1,128)S(1)}, u32[]{:S(2)}, u32[]{:S(2)}) async-start(f32[16,1,1024]{2,1,0:T(1,128)} %all_to_all.30), calls=%async_computation.4 | async-start | bytes 131072 | tf_op jit(solution)/shard_map/all_to_all | solution.py:159
  136.4 5.3 %collective-permute-start.1 = (f32[4096]{0:T(1024)S(1)}, f32[4096]{0:T(1024)S(1)}, u32[]{:S(2)}, u32[]{:S(2)}) collective-permute-start(f32[4096]{0:T(1024)S(1)} %get-tuple-element.3), channel_id=1, source_target_pairs={{0,128},{128,0},{1,129},{129,1},{2,130},{130,2},{3,131},{131,3},{4... | collective-permute-start | bytes 49160 | tf_op jit(solution)/shard_map/ppermute | solution.py:151
  141.7 0.6 fusion.6
  142.3 2.0 %collective-permute-done.1 = f32[4096]{0:T(1024)S(1)} collective-permute-done((f32[4096]{0:T(1024)S(1)}, f32[4096]{0:T(1024)S(1)}, u32[]{:S(2)}, u32[]{:S(2)}) %collective-permute-start.1) | collective-permute-done | bytes 16416 | tf_op jit(solution)/shard_map/ppermute | solution.py:151
  144.3 0.6 maximum_select_fusion
  145.0 0.6 broadcast_multiply_fusion.1
  (18 shorter events, 0.4 us)
Async XLA Ops:
  28.8 32.2 %all-to-all-start.1 = ((bf16[16,256,256]{2,1,0:T(8,128)(2,1)}), bf16[16,256,256]{2,1,0:T(8,128)(2,1)S(1)}, u32[]{:S(2)}, u32[]{:S(2)}) async-start(bf16[16,256,256]{2,1,0:T(8,128)(2,1)} %broadcast_in_dim.17), calls=%async_computation.1 | async-start | bytes 4194304 | tf_op jit(solution)/shard_map/all_to_all | solution.py:111
  35.5 4.4 %collective-permute-start = (bf16[8,128,256]{2,1,0:T(8,128)(2,1)S(1)}, bf16[8,128,256]{2,1,0:T(8,128)(2,1)S(1)}, u32[]{:S(2)}, u32[]{:S(2)}) collective-permute-start(bf16[8,128,256]{2,1,0:T(8,128)(2,1)S(1)} %all_to_all.37), channel_id=1, source_target_pairs={{0,1},{1,0},{2,3},{3,2},{4,5},{5,4},{6,7},{7,6},{8,9},{9,8},{10,11... | collective-permute-start | bytes 1572872 | tf_op jit(solution)/shard_map/ppermute | solution.py:126
  40.0 0.8 copy-start
  40.0 1.0 copy-start.1
  41.0 20.7 %copy-start.2 = (f32[8192]{0:T(1024)S(1)}, f32[8192]{0:T(1024)}, u32[]{:S(2)}) copy-start(f32[8192]{0:T(1024)} %param.5) | copy-start | bytes 98308
  72.9 18.5 %all-to-all-start.2 = ((f32[16,1,2048]{2,1,0:T(1,128)}), f32[16,1,2048]{2,1,0:T(1,128)S(1)}, u32[]{:S(2)}, u32[]{:S(2)}) async-start(f32[16,1,2048]{2,1,0:T(1,128)} %broadcast_in_dim.19), calls=%async_computation.2 | async-start | bytes 262144 | tf_op jit(solution)/shard_map/all_to_all | solution.py:111
  105.1 12.6 %all-to-all-start.3 = ((f32[16,1,4096]{2,1,0:T(1,128)}), f32[16,1,4096]{2,1,0:T(1,128)S(1)}, u32[]{:S(2)}, u32[]{:S(2)}) async-start(f32[16,1,4096]{2,1,0:T(1,128)} %broadcast_in_dim.20), calls=%async_computation.3 | async-start | bytes 524288 | tf_op jit(solution)/shard_map/all_to_all | solution.py:111
  132.5 12.4 %all-to-all-start.4 = ((f32[16,1,1024]{2,1,0:T(1,128)}), f32[16,1,1024]{2,1,0:T(1,128)S(1)}, u32[]{:S(2)}, u32[]{:S(2)}) async-start(f32[16,1,1024]{2,1,0:T(1,128)} %all_to_all.30), calls=%async_computation.4 | async-start | bytes 131072 | tf_op jit(solution)/shard_map/all_to_all | solution.py:159
  136.4 7.9 %collective-permute-start.1 = (f32[4096]{0:T(1024)S(1)}, f32[4096]{0:T(1024)S(1)}, u32[]{:S(2)}, u32[]{:S(2)}) collective-permute-start(f32[4096]{0:T(1024)S(1)} %get-tuple-element.3), channel_id=1, source_target_pairs={{0,128},{128,0},{1,129},{129,1},{2,130},{130,2},{3,131},{131,3},{4... | collective-permute-start | bytes 49160 | tf_op jit(solution)/shard_map/ppermute | solution.py:151

commit v2 on v1

v2 whole, which is shorter than its diff:
```python
import functools
import math

import jax
import jax.numpy as jnp
from jax import lax
from jax.experimental import pallas as pl
from jax.experimental.pallas import tpu as pltpu
from jax.sharding import Mesh
from jax.sharding import PartitionSpec as P

EPS = 0.01
AXES = ("zh", "y", "x", "zl", "core")
ROW_GROUP = ("zh", "zl", "core")
COL_GROUP = ("y", "x")
LN2 = math.log(2.0)
LOG2E = 1.0 / LN2


def nt_dot(a, b):
    return lax.dot_general(a, b, (((1,), (1,)), ((), ())), preferred_element_type=jnp.float32)


SAMPLE = 16

def lse_kernel(scale, width, copies, x_ref, y_ref, bias_ref, few_ref, out_ref):
    tm, cols = x_ref.shape[0], y_ref.shape[0]
    x = x_ref[...]
    step = cols // 16
    few = jnp.concatenate([y_ref[s : s + SAMPLE, :] for s in range(0, cols, step)], axis=0)
    seen = nt_dot(x, few)
    seen = jnp.maximum(seen[:, :128] * scale + few_ref[:, :128], seen[:, 128:] * scale + few_ref[:, 128:])
    base = jnp.max(seen, axis=1, keepdims=True)
    wide = jnp.broadcast_to(base, (tm, 128))
    total = jnp.zeros((tm, 128), jnp.float32)
    for start in range(0, cols, width):
        prod = nt_dot(x, y_ref[start : start + width, :])
        for o in range(0, width, 128):
            total = total + jnp.exp2(
                (prod[:, o : o + 128] * scale + bias_ref[:, start + o : start + o + 128]) - wide
            )
    total = jnp.sum(total, axis=1, keepdims=True)
    value = jnp.broadcast_to(base + jnp.log2(total), (tm, 128)).T
    out_ref[...] = jnp.broadcast_to(value[None, :1], (copies, 1, tm))

    @pl.when(jnp.logical_not(jnp.max(total) < 1e36))
    def _():
        def rows(r, _):
            own = pl.ds(pl.multiple_of(r * 128, 128), 128)
            xs = x_ref[own, :]

            def columns(c, state):
                top, total = state
                at = pl.multiple_of(c * 128, 128)
                part = nt_dot(xs, y_ref[pl.ds(at, 128), :]) * scale + bias_ref[:, pl.ds(at, 128)]
                new = jnp.maximum(top, part)
                return new, total * jnp.exp2(top - new) + jnp.exp2(part - new)

            state = jnp.full((128, 128), -1e38, jnp.float32), jnp.zeros((128, 128), jnp.float32)
            top, total = lax.fori_loop(0, cols // 128, columns, state)
            best = jnp.max(top, axis=1, keepdims=True)
            total = jnp.sum(total * jnp.exp2(top - best), axis=1, keepdims=True)
            value = jnp.broadcast_to(best + jnp.log2(total), (128, 128)).T
            out_ref[:, :, own] = jnp.broadcast_to(value[None, :1], (copies, 1, 128))
            return 0

        lax.fori_loop(0, tm // 128, rows, 0)


def lse(x, y, bias, scale, copies=16, tm=1024, width=256):
    rows, depth = x.shape
    cols = y.shape[0]
    few = bias.reshape(16, cols // 16)[:, :SAMPLE].reshape(1, 16 * SAMPLE)
    return pl.pallas_call(
        functools.partial(lse_kernel, scale, width, copies),
        grid=(rows // tm,),
        in_specs=[
            pl.BlockSpec((tm, depth), lambda i: (i, 0)),
            pl.BlockSpec((cols, depth), lambda i: (0, 0)),
            pl.BlockSpec((1, cols), lambda i: (0, 0)),
            pl.BlockSpec((1, 16 * SAMPLE), lambda i: (0, 0)),
        ],
        out_specs=pl.BlockSpec((copies, 1, tm), lambda i: (0, 0, i)),
        out_shape=jax.ShapeDtypeStruct((copies, 1, rows), jnp.float32),
        compiler_params=pltpu.CompilerParams(vmem_limit_bytes=40 * 2**20),
        cost_estimate=pl.CostEstimate(
            flops=2 * rows * cols * depth, bytes_accessed=2 * depth * (rows + cols), transcendentals=rows * cols
        ),
    )(x, y, bias.reshape(1, cols), few)


def reward_kernel(scale, width, x_ref, y_ref, rbias_ref, rsq_ref, cbias_ref, csq_ref, out_ref):
    x = x_ref[...]
    tm = x.shape[0]
    rbias = jnp.broadcast_to(rbias_ref[...], (128, tm)).T
    mass = jnp.zeros((tm, 128), jnp.float32)
    moment = jnp.zeros((tm, 128), jnp.float32)
    for start in range(0, y_ref.shape[0], width):
        prod = nt_dot(x, y_ref[start : start + width, :])
        for o in range(0, width, 128):
            part = prod[:, o : o + 128]
            cols = slice(start + o, start + o + 128)
            plan = jnp.exp2((part * scale + cbias_ref[:, cols]) + rbias)
            mass = mass + plan
            moment = moment + plan * (part - csq_ref[:, cols])
    mass = jnp.broadcast_to(jnp.sum(mass, axis=1, keepdims=True), (tm, 128)).T[:1]
    moment = jnp.broadcast_to(jnp.sum(moment, axis=1, keepdims=True), (tm, 128)).T[:1]
    half = tm // 2
    value = rsq_ref[...] * mass - 2.0 * moment
    out_ref[:8] = jnp.broadcast_to(value[None, :, :half], (8, 1, half))
    out_ref[8:] = jnp.broadcast_to(value[None, :, half:], (8, 1, half))


def reward_part(x, y, rbias, rsq, cbias, csq, scale, width=256):
    rows, depth = x.shape
    cols = y.shape[0]
    return pl.pallas_call(
        functools.partial(reward_kernel, scale, width),
        out_shape=jax.ShapeDtypeStruct((16, 1, rows // 2), jnp.float32),
        compiler_params=pltpu.CompilerParams(vmem_limit_bytes=40 * 2**20),
        cost_estimate=pl.CostEstimate(
            flops=2 * rows * cols * depth, bytes_accessed=2 * depth * (rows + cols), transcendentals=rows * cols
        ),
    )(x, y, rbias, rsq, cbias, csq)


def copy_kernel(in_ref, out_ref):
    out_ref[...] = in_ref[...][None]


def share(a, axes):
    n = math.prod(lax.axis_size(ax) for ax in axes)
    many = pl.pallas_call(
        copy_kernel,
        grid=(n,),
        in_specs=[pl.BlockSpec(a.shape, lambda i: (0, 0))],
        out_specs=pl.BlockSpec((1,) + a.shape, lambda i: (i, 0, 0)),
        out_shape=jax.ShapeDtypeStruct((n,) + a.shape, a.dtype),
    )(a)
    return lax.all_to_all(many, axes, 0, 0)


def swap(a, axis, bit, before):
    size = lax.axis_size(axis)
    other = lax.ppermute(a, axis, [(i, i ^ bit) for i in range(size)])
    low = (lax.axis_index(axis) & bit) == 0
    return jnp.stack([jnp.where(low, a, other), jnp.where(low, other, a)], axis=before)


def merge(parts):
    parts = parts[:, 0]
    best = jnp.max(parts, axis=0)
    return best + jnp.log2(jnp.sum(jnp.exp2(parts - best), axis=0))


def body(logged, fresh, warm):
    depth = logged.shape[1]
    zh = lax.axis_index("zh")
    n_rows = logged.shape[0] * 256
    n_cols = fresh.shape[0] * 256

    y = share(fresh, COL_GROUP).reshape(-1, depth)
    x = swap(logged, "zh", 1, 0)
    x = swap(x, "zl", 2, 1)
    x = swap(x, "zl", 1, 2)
    x = swap(x, "core", 1, 3).reshape(-1, depth)
    rows, cols = x.shape[0], y.shape[0]

    scale = 2.0 * LOG2E / (depth * EPS)
    xw = x.astype(jnp.float32)
    xsq = jnp.sum(xw * xw, axis=1)
    yw = y.astype(jnp.float32)
    ysq = jnp.sum(yw * yw, axis=1)
    warm = lax.dynamic_slice(warm, (zh * cols,), (cols,))

    bias = warm * (LOG2E / EPS) - ysq * (0.5 * scale)
    part = lse(x, y, bias, scale, tm=rows)
    total = merge(lax.all_to_all(part, ROW_GROUP, 0, 0))
    rbias = -total - math.log2(n_rows)
    row_all = (rbias + xsq * (0.5 * scale)) * (EPS * LN2)

    part = lse(y, x, rbias, scale, tm=cols)
    total = merge(lax.all_to_all(part, COL_GROUP, 0, 0))
    cbias = -total - math.log2(n_cols)
    col_half = (cbias + ysq * (0.5 * scale)) * (EPS * LN2)
    theirs = lax.ppermute(col_half, "zh", [(0, 1), (1, 0)])
    col_potential = jnp.where(
        zh == 0, jnp.concatenate([col_half, theirs]), jnp.concatenate([theirs, col_half])
    )

    part = reward_part(x, y, rbias[None], xsq[None], cbias[None], (0.5 * ysq)[None], scale)
    got = lax.all_to_all(part, ROW_GROUP, 0, 0)
    reward = jnp.sum(got[:, 0], axis=0) * (-n_rows / depth)
    row_potential = lax.dynamic_slice(row_all, (zh * (rows // 2),), (rows // 2,))
    return row_potential, col_potential, reward


def solution(mesh):
    fine = Mesh(mesh.devices.reshape(2, 4, 4, 4, 2), AXES)
    return jax.shard_map(
        body,
        mesh=fine,
        in_specs=(P(AXES, None), P(("zl", "core", "zh", "y", "x"), None), P(("zl", "core"))),
        out_specs=(P(("zh", "y", "x")), P(("zl", "core")), P(("zh", "y", "x"))),
        check_vma=False,
    )
```

time: 146 us -> 329 us (2.25)
  starting transfers between devices: 31.6 us -> 143 us
  Pallas kernels: 35.6 us -> 134 us
  blocking collectives: 24.8 us -> 0 us
  local copies, waits for them, and re-layouts: 7.17 us -> 1.17 us
    all_to_all x4, starting transfers between devices: 23.5 us -> 127 us  [the longest x1 104 us: body(): total = merge(lax.all_to_all(part, ROW_GROUP, 0, 0))]
    pallas_call x3 -> x4, Pallas kernels: 35.6 us -> 134 us  [the longest x2 117 us: lse(): pl.pallas_call(functools.partial(lse_kernel, scale, width, copies), grid=...]
    all_to_all x1 -> x0, blocking collectives: 24.8 us -> none  [share(): return lax.all_to_all(jnp.broadcast_to(a[None], (n,) + a.shape), axes, 0, 0)]
    ppermute x1 -> x4, starting transfers between devices: 2.82 us -> 15.4 us  [swap(): other = lax.ppermute(a, axis, [(i, i ^ bit) for i in range(size)])]
    ppermute x1 -> x4, waiting for transfers between devices: 1.54 us -> 7.48 us  [swap(): other = lax.ppermute(a, axis, [(i, i ^ bit) for i in range(size)])]
    broadcast_in_dim x6 -> x0, local copies, waits for them, and re-layouts: 4.95 us -> none  [the longest x4 4.93 us: share(): return lax.all_to_all(jnp.broadcast_to(a[None], (n,) + a.shape), axes, 0, 0)]
    ppermute x1, starting transfers between devices: 5.34 us -> 0.46 us  [body(): theirs = lax.ppermute(col_half, 'zh', [(0, 1), (1, 0)])]
  transfers between devices with their start and end apart: 6 -> 9, of which waited for: 5 -> 7; matrix products, arithmetic and copies ran while one was open for 2% -> 1% of each run, Pallas kernels for 0% -> 5%
where the time goes in v2:
time: 329 us; the launch traced here: 327 us
  starting transfers between devices  143 us (43%)
  Pallas kernels  134 us (41%)
  waiting for transfers between devices  41.3 us (13%)
  other arithmetic  6.59 us (2%)
    pallas_call x2, Pallas kernels, lse(): pl.pallas_call(functools.partial(lse_kernel, scale, width, copies), grid=...  117 us
    all_to_all x1, starting transfers between devices, body(): total = merge(lax.all_to_all(part, ROW_GROUP, 0, 0))  104 us
    ppermute x4, starting transfers between devices, swap(): other = lax.ppermute(a, axis, [(i, i ^ bit) for i in range(size)])  15.4 us
    all_to_all x1, waiting for transfers between devices, share(): return lax.all_to_all(many, axes, 0, 0)  11.1 us
    pallas_call x1, Pallas kernels, reward_part(): pl.pallas_call(functools.partial(reward_kernel, scale, width), out_shape=...  10.9 us
    all_to_all x1, waiting for transfers between devices, body(): total = merge(lax.all_to_all(part, ROW_GROUP, 0, 0))  9.17 us
    all_to_all x1, starting transfers between devices, body(): total = merge(lax.all_to_all(part, COL_GROUP, 0, 0))  8.32 us
    all_to_all x1, starting transfers between devices, body(): got = lax.all_to_all(part, ROW_GROUP, 0, 0)  8.12 us
  transfers between devices with their start and end apart: 9, of which 7 were waited for; matrix products, arithmetic and copies ran while one was open for 1% of the time, Pallas kernels for 5%

profile of v2, /device:TPU:1, one launch (start us, length us, event | category | flops | bytes accessed | tf_op | source)
XLA Modules:
  0.0 327.1 jit_solution(5739095938928465352)
XLA Ops:
  0.6 7.8 %collective-permute-start = (bf16[128,256]{1,0:T(8,128)(2,1)}, bf16[128,256]{1,0:T(8,128)(2,1)S(1)}, u32[]{:S(2)}, u32[]{:S(2)}) collective-permute-start(bf16[128,256]{1,0:T(8,128)(2,1)} %param.3), channel_id=1, source_target_pairs={{0,128},{128,0},{1,129},{129,1},{2,130},{130,2},{3,131},{131,3},{4... | collective-permute-start | bytes 196616 | tf_op jit(solution)/shard_map/ppermute | solution.py:145
  8.5 2.0 collective-permute-done
  10.4 0.9 select_bitcast_fusion.7
  11.3 1.4 collective-permute-start.1
  12.7 6.2 %shard_map.58 = bf16[16,256,256]{2,1,0:T(8,128)(2,1)} custom-call(bf16[256,256]{1,0:T(8,128)(2,1)} %in_ref.1), custom_call_target="tpu_custom_call" | custom-call | tf_op jit(solution)/shard_map/pallas_call | solution.py:133
  19.0 6.8 %all-to-all-start = ((bf16[16,256,256]{2,1,0:T(8,128)(2,1)}), bf16[16,256,256]{2,1,0:T(8,128)(2,1)S(1)}, u32[]{:S(2)}, u32[]{:S(2)}) async-start(bf16[16,256,256]{2,1,0:T(8,128)(2,1)} %shard_map.58), calls=%async_computation | async-start | bytes 4194304 | tf_op jit(solution)/shard_map/all_to_all | solution.py:140
  25.8 1.7 collective-permute-start.2
  27.5 3.8 %collective-permute-done.2 = bf16[2,2,128,256]{3,2,0,1:T(8,128)(2,1)S(1)} collective-permute-done((bf16[2,2,128,256]{3,2,0,1:T(8,128)(2,1)S(1)}, bf16[2,2,128,256]{3,2,0,1:T(8,128)(2,1)S(1)}, u32[]{:S(2)}, u32[]{:S(2)}) %collective-permute-start.2) | collective-permute-done | bytes 262176 | tf_op jit(solution)/shard_map/ppermute | solution.py:145
  31.3 0.8 pad_maximum_fusion.1
  32.2 4.4 %collective-permute-start.3 = (bf16[2,2,2,128,256]{4,3,0,1,2:T(8,128)(2,1)}, bf16[2,2,2,128,256]{4,3,0,1,2:T(8,128)(2,1)S(1)}, u32[]{:S(2)}, u32[]{:S(2)}) collective-permute-start(bf16[2,2,2,128,256]{4,3,0,1,2:T(8,128)(2,1)} %pad_maximum_fusion.1), channel_id=1, source_target_pairs={{0,1},{1,0},{2,3},{3,2},{4,5},{5,4},{6,7},{7,6},{8,9},{9,8},{10,11... | collective-permute-start | bytes 1572872 | tf_op jit(solution)/shard_map/ppermute | solution.py:145
  36.6 1.7 collective-permute-done.3
  38.5 0.1 pad_maximum_fusion
  38.6 0.7 copy-done
  39.2 0.2 copy-done.1
  39.5 11.1 %all-to-all-done = bf16[16,256,256]{2,1,0:T(8,128)(2,1)S(1)} async-done(((bf16[16,256,256]{2,1,0:T(8,128)(2,1)}), bf16[16,256,256]{2,1,0:T(8,128)(2,1)S(1)}, u32[]{:S(2)}, u32[]{:S(2)}) %all-to-all-start) | async-done | bytes 2097184 | tf_op jit(solution)/shard_map/all_to_all | solution.py:140
  50.6 0.6 multiply_reduce_fusion
  51.4 7.3 %shard_map.59 = f32[16,1,2048]{2,1,0:T(1,128)} custom-call(bf16[2048,256]{1,0:T(8,128)(2,1)S(1)} %bitcast.51, bf16[4096,256]{1,0:T(8,128)(2,1)S(1)} %bitcast.48, f32[1,4096]{1,0:T(1,128)S(1)} %bitcast.54, f32[1,256]{1,0:T(1,128)S(1)} %reshape.115.few_ref), custom_call_target="tpu_custom_call" | custom-call | flops 4294967296 | bytes 3145728 | tf_op jit(solution)/shard_map/pallas_call | solution.py:74
  58.7 103.7 %all-to-all-start.1 = ((f32[16,1,2048]{2,1,0:T(1,128)}), f32[16,1,2048]{2,1,0:T(1,128)S(1)}, u32[]{:S(2)}, u32[]{:S(2)}) async-start(f32[16,1,2048]{2,1,0:T(1,128)} %shard_map.59), calls=%async_computation.1 | async-start | bytes 262144 | tf_op jit(solution)/shard_map/all_to_all | solution.py:178
  162.4 9.2 %all-to-all-done.1 = f32[16,1,2048]{2,1,0:T(1,128)S(1)} async-done(((f32[16,1,2048]{2,1,0:T(1,128)}), f32[16,1,2048]{2,1,0:T(1,128)S(1)}, u32[]{:S(2)}, u32[]{:S(2)}) %all-to-all-start.1) | async-done | bytes 131104 | tf_op jit(solution)/shard_map/all_to_all | solution.py:178
  171.9 110.0 %shard_map.60 = f32[16,1,4096]{2,1,0:T(1,128)} custom-call(bf16[4096,256]{1,0:T(8,128)(2,1)S(1)} %bitcast.49, bf16[2048,256]{1,0:T(8,128)(2,1)S(1)} %bitcast.52, f32[1,2048]{1,0:T(1,128)S(1)} %bitcast.56, f32[1,256]{1,0:T(1,128)S(1)} %reshape.116.few_ref), custom_call_target="tpu_custom_call" | custom-call | flops 4294967296 | bytes 3145728 | tf_op jit(solution)/shard_map/pallas_call | solution.py:74
  281.9 8.3 %all-to-all-start.2 = ((f32[16,1,4096]{2,1,0:T(1,128)}), f32[16,1,4096]{2,1,0:T(1,128)S(1)}, u32[]{:S(2)}, u32[]{:S(2)}) async-start(f32[16,1,4096]{2,1,0:T(1,128)} %shard_map.60), calls=%async_computation.2 | async-start | bytes 524288 | tf_op jit(solution)/shard_map/all_to_all | solution.py:183
  290.2 1.6 multiply_reduce_fusion.1
  291.8 7.0 %all-to-all-done.2 = f32[16,1,4096]{2,1,0:T(1,128)S(1)} async-done(((f32[16,1,4096]{2,1,0:T(1,128)}), f32[16,1,4096]{2,1,0:T(1,128)S(1)}, u32[]{:S(2)}, u32[]{:S(2)}) %all-to-all-start.2) | async-done | bytes 262176 | tf_op jit(solution)/shard_map/all_to_all | solution.py:183
  298.8 0.2 reduce_max.19
  299.0 0.2 fusion.2
  299.2 0.5 collective-permute-start.4
  299.7 10.9 %shard_map.61 = f32[16,1,1024]{2,1,0:T(1,128)} custom-call(bf16[2048,256]{1,0:T(8,128)(2,1)S(1)} %bitcast.53, bf16[4096,256]{1,0:T(8,128)(2,1)S(1)} %bitcast.50, f32[1,2048]{1,0:T(1,128)S(1)} %bitcast.57, f32[1,2048]{1,0:T(1,128)S(1)} %bitcast.60, f32[1,4096]{1,0:T(1,128)S(1)} %bitcast.58, f32[1,4096]{1,0:T(1,128)S(1)} %bitcast.59), custom_call_target="tpu_custom_call" | custom-call | flops 4294967296 | bytes 3145728 | tf_op jit(solution)/shard_map/pallas_call | solution.py:117
  310.6 8.1 %all-to-all-start.3 = ((f32[16,1,1024]{2,1,0:T(1,128)}), f32[16,1,1024]{2,1,0:T(1,128)S(1)}, u32[]{:S(2)}, u32[]{:S(2)}) async-start(f32[16,1,1024]{2,1,0:T(1,128)} %shard_map.61), calls=%async_computation.3 | async-start | bytes 131072 | tf_op jit(solution)/shard_map/all_to_all | solution.py:192
  318.7 0.6 fusion.6
  319.3 0.6 maximum_select_fusion
  319.9 6.6 %all-to-all-done.3 = f32[16,1,1024]{2,1,0:T(1,128)S(1)} async-done(((f32[16,1,1024]{2,1,0:T(1,128)}), f32[16,1,1024]{2,1,0:T(1,128)S(1)}, u32[]{:S(2)}, u32[]{:S(2)}) %all-to-all-start.3) | async-done | bytes 65568 | tf_op jit(solution)/shard_map/all_to_all | solution.py:192
  326.5 0.6 broadcast_multiply_fusion.1
  (28 shorter events, 0.8 us)
Async XLA Ops:
  0.6 9.8 %collective-permute-start = (bf16[128,256]{1,0:T(8,128)(2,1)}, bf16[128,256]{1,0:T(8,128)(2,1)S(1)}, u32[]{:S(2)}, u32[]{:S(2)}) collective-permute-start(bf16[128,256]{1,0:T(8,128)(2,1)} %param.3), channel_id=1, source_target_pairs={{0,128},{128,0},{1,129},{129,1},{2,130},{130,2},{3,131},{131,3},{4... | collective-permute-start | bytes 196616 | tf_op jit(solution)/shard_map/ppermute | solution.py:145
  11.3 14.4 %collective-permute-start.1 = (bf16[2,128,256]{2,1,0:T(8,128)(2,1)S(1)}, bf16[2,128,256]{2,1,0:T(8,128)(2,1)S(1)}, u32[]{:S(2)}, u32[]{:S(2)}) collective-permute-start(bf16[2,128,256]{2,1,0:T(8,128)(2,1)S(1)} %pad_maximum_fusion.3), channel_id=1, source_target_pairs={{0,4},{2,6},{4,0},{6,2},{1,5},{3,7},{5,1},{7,3},{8,12},{10,14},{12... | collective-permute-start | bytes 393224 | tf_op jit(solution)/shard_map/ppermute | solution.py:145
  19.0 31.6 %all-to-all-start = ((bf16[16,256,256]{2,1,0:T(8,128)(2,1)}), bf16[16,256,256]{2,1,0:T(8,128)(2,1)S(1)}, u32[]{:S(2)}, u32[]{:S(2)}) async-start(bf16[16,256,256]{2,1,0:T(8,128)(2,1)} %shard_map.58), calls=%async_computation | async-start | bytes 4194304 | tf_op jit(solution)/shard_map/all_to_all | solution.py:140
  25.8 5.5 %collective-permute-start.2 = (bf16[2,2,128,256]{3,2,0,1:T(8,128)(2,1)S(1)}, bf16[2,2,128,256]{3,2,0,1:T(8,128)(2,1)S(1)}, u32[]{:S(2)}, u32[]{:S(2)}) collective-permute-start(bf16[2,2,128,256]{3,2,0,1:T(8,128)(2,1)S(1)} %pad_maximum_fusion.2), channel_id=1, source_target_pairs={{0,2},{2,0},{4,6},{6,4},{1,3},{3,1},{5,7},{7,5},{8,10},{10,8},{12,... | collective-permute-start | bytes 786440 | tf_op jit(solution)/shard_map/ppermute | solution.py:145
  32.2 6.2 %collective-permute-start.3 = (bf16[2,2,2,128,256]{4,3,0,1,2:T(8,128)(2,1)}, bf16[2,2,2,128,256]{4,3,0,1,2:T(8,128)(2,1)S(1)}, u32[]{:S(2)}, u32[]{:S(2)}) collective-permute-start(bf16[2,2,2,128,256]{4,3,0,1,2:T(8,128)(2,1)} %pad_maximum_fusion.1), channel_id=1, source_target_pairs={{0,1},{1,0},{2,3},{3,2},{4,5},{5,4},{6,7},{7,6},{8,9},{9,8},{10,11... | collective-permute-start | bytes 1572872 | tf_op jit(solution)/shard_map/ppermute | solution.py:145
  38.4 0.8 copy-start
  38.4 1.0 copy-start.1
  39.4 11.8 %copy-start.2 = (f32[8192]{0:T(1024)S(1)}, f32[8192]{0:T(1024)}, u32[]{:S(2)}) copy-start(f32[8192]{0:T(1024)} %param.5) | copy-start | bytes 98308
  58.7 112.9 %all-to-all-start.1 = ((f32[16,1,2048]{2,1,0:T(1,128)}), f32[16,1,2048]{2,1,0:T(1,128)S(1)}, u32[]{:S(2)}, u32[]{:S(2)}) async-start(f32[16,1,2048]{2,1,0:T(1,128)} %shard_map.59), calls=%async_computation.1 | async-start | bytes 262144 | tf_op jit(solution)/shard_map/all_to_all | solution.py:178
  281.9 16.9 %all-to-all-start.2 = ((f32[16,1,4096]{2,1,0:T(1,128)}), f32[16,1,4096]{2,1,0:T(1,128)S(1)}, u32[]{:S(2)}, u32[]{:S(2)}) async-start(f32[16,1,4096]{2,1,0:T(1,128)} %shard_map.60), calls=%async_computation.2 | async-start | bytes 524288 | tf_op jit(solution)/shard_map/all_to_all | solution.py:183
  299.2 20.1 %collective-permute-start.4 = (f32[4096]{0:T(1024)S(1)}, f32[4096]{0:T(1024)S(1)}, u32[]{:S(2)}, u32[]{:S(2)}) collective-permute-start(f32[4096]{0:T(1024)S(1)} %get-tuple-element.3), channel_id=1, source_target_pairs={{0,128},{128,0},{1,129},{129,1},{2,130},{130,2},{3,131},{131,3},{4... | collective-permute-start | bytes 49160 | tf_op jit(solution)/shard_map/ppermute | solution.py:186
  310.6 15.9 %all-to-all-start.3 = ((f32[16,1,1024]{2,1,0:T(1,128)}), f32[16,1,1024]{2,1,0:T(1,128)S(1)}, u32[]{:S(2)}, u32[]{:S(2)}) async-start(f32[16,1,1024]{2,1,0:T(1,128)} %shard_map.61), calls=%async_computation.3 | async-start | bytes 131072 | tf_op jit(solution)/shard_map/all_to_all | solution.py:192
